TPU v7x, 32 devices: a whole 2x2x4 slice. The times are simulated.
32 devices in a mesh: lat: 4 (over x, core), lon: 8 (over z, y).
Axes of the slice: x: 2, y: 2, z: 4, core: 2. Of those that a mesh axis runs over, the one named last changes fastest.
Arguments:
- prior_ensemble: bfloat16 [3, 128, 8, 1024], P(None, None, 'lat', 'lon'), may hold values from -6 to 6
- observed: float32 [4, 8, 256], P('lat', 'lon'), may hold values from -6 to 6
- obs_error: float32 [4, 8, 256], P('lat', 'lon'), may hold values from 0.2 to 80
- obs_index: int32 [4, 8, 256], P('lat', 'lon'), may hold values from 0 to 767
- obs_count: int32 [4, 8], P('lat', 'lon'), may hold values from 128 to 256, as said below
Outputs:
- posterior_ensemble: float32 [3, 128, 8, 1024], P(None, None, 'lat', 'lon')
Inputs may be any that keep to these rules, and one draw needn't show every extreme that they name: `obs_count`: every tile has between 128 and 256 live slots; some tile has all 256.
All inputs are finite; a program needn't handle non-finite values.
Results may differ from a plain program's by a relative error of at most 0.0003.
Values sent between devices are 32-bit elements; how exact they have to be, the bound alone decides.
A program may use at most 128 MiB of HBM per device.

v0:
```python
import math

import jax
import jax.numpy as jnp
from jax import lax
from jax.sharding import PartitionSpec as P

HALF_COURANT = 0.4
ROTATION = 0.8
BAND = math.pi / 6.0


def with_halo(block, sides, width, periodic):
    for axis, dim in sides:
        count = lax.axis_size(axis)
        forward = [(i, i + 1) for i in range(count - 1)]
        if periodic:
            forward.append((count - 1, 0))
        backward = [(target, source) for source, target in forward]
        low = lax.ppermute(
            lax.slice_in_dim(block, block.shape[dim] - width, None, axis=dim), axis, forward
        )
        high = lax.ppermute(lax.slice_in_dim(block, 0, width, axis=dim), axis, backward)
        block = jnp.concatenate([low, block, high], axis=dim)
    return block


def rotation_rows(first_row, count, total_rows):
    rows = first_row + jnp.arange(count, dtype=jnp.int32)
    latitude = BAND * (2.0 * (rows.astype(jnp.float32) + 0.5) / total_rows - 1.0)
    return (ROTATION * jnp.sin(latitude))[:, None]


def tendency(padded, rotation):
    height, zonal_wind, merid_wind = (padded[0], padded[1], padded[2])
    d_height = -HALF_COURANT * (
        zonal_wind[..., 1:-1, 2:]
        - zonal_wind[..., 1:-1, :-2]
        + (merid_wind[..., 2:, 1:-1] - merid_wind[..., :-2, 1:-1])
    )
    d_zonal = (
        -HALF_COURANT * (height[..., 1:-1, 2:] - height[..., 1:-1, :-2])
        + rotation * merid_wind[..., 1:-1, 1:-1]
    )
    d_merid = (
        -HALF_COURANT * (height[..., 2:, 1:-1] - height[..., :-2, 1:-1])
        - rotation * zonal_wind[..., 1:-1, 1:-1]
    )
    return jnp.stack([d_height, d_zonal, d_merid], axis=0)


def shards(prior_ensemble, observed, obs_error, obs_index, obs_count):
    system_vector = prior_ensemble.astype(jnp.float32)
    ensemble_vectors = system_vector.shape[1]
    lat_rows = system_vector.shape[2]
    lon_cols = system_vector.shape[3]
    total_rows = lat_rows * lax.axis_size("lat")
    first_row = lax.axis_index("lat") * lat_rows
    inner_rotation = rotation_rows(first_row, lat_rows, total_rows)
    padded = with_halo(system_vector, (("lat", 2),), 2, False)
    padded = with_halo(padded, (("lon", 3),), 2, True)
    outer_rotation = rotation_rows(first_row - 1, lat_rows + 2, total_rows)
    wide_rate = tendency(padded, outer_rotation)
    outer_rows = first_row - 1 + jnp.arange(lat_rows + 2, dtype=jnp.int32)
    inside = ((outer_rows >= 0) & (outer_rows < total_rows)).astype(jnp.float32)[:, None]
    wide_mid = (padded[:, :, 1:-1, 1:-1] + wide_rate) * inside
    upper_coefficient = wide_rate[:, :, 1:-1, 1:-1]
    lower_coefficient = tendency(wide_mid, inner_rotation)
    predicted_ensemble = system_vector + 0.5 * (upper_coefficient + lower_coefficient)
    mesh_points = lat_rows * lon_cols
    unrolled_vector = predicted_ensemble.reshape(3, ensemble_vectors, mesh_points)
    index_list = obs_index.reshape(-1)
    slot_total = index_list.shape[0]
    variable_slot = index_list // mesh_points
    cell_index = index_list % mesh_points
    measured_vector = unrolled_vector[variable_slot, :, cell_index]
    state_mean = jnp.mean(measured_vector, axis=-1)
    live = (jnp.arange(slot_total, dtype=jnp.int32) < obs_count.reshape(())).astype(jnp.float32)
    weight_rows = live / obs_error.reshape(-1)
    scaled = (measured_vector - state_mean[:, None]) * weight_rows[:, None]
    innovation = (observed.reshape(-1) - state_mean) * weight_rows
    local_gram = jnp.dot(scaled.T, scaled, precision=lax.Precision.HIGHEST)
    local_push = jnp.dot(innovation, scaled, precision=lax.Precision.HIGHEST)
    identity = jnp.eye(ensemble_vectors, dtype=jnp.float32)
    prior = float(ensemble_vectors - 1)
    gram, push = lax.psum((local_gram, local_push), ("lat", "lon"))
    factor = jnp.linalg.cholesky(prior * identity + gram)
    inverse = lax.linalg.triangular_solve(factor, identity, left_side=True, lower=True)
    transform = math.sqrt(prior) * inverse.T
    forward = lax.linalg.triangular_solve(factor, push[:, None], left_side=True, lower=True)
    mean_weights = lax.linalg.triangular_solve(
        factor, forward, left_side=True, lower=True, transpose_a=True
    )
    weights = transform + mean_weights
    state_center = jnp.mean(unrolled_vector, axis=1, keepdims=True)
    anomaly = unrolled_vector - state_center
    posterior_ensemble = state_center + jnp.einsum(
        "fic,ij->fjc", anomaly, weights, precision=lax.Precision.HIGHEST
    )
    return posterior_ensemble.reshape(predicted_ensemble.shape)


def solution(mesh):
    placed = (
        P(None, None, "lat", "lon"),
        P("lat", "lon", None),
        P("lat", "lon", None),
        P("lat", "lon", None),
        P("lat", "lon"),
    )
    return jax.shard_map(
        shards, mesh=mesh, in_specs=placed, out_specs=P(None, None, "lat", "lon"), check_vma=False
    )
```

profile of v0, /device:TPU:0, one launch (start us, length us, event | category | flops | bytes accessed | tf_op | source)
XLA Modules:
  0.0 183.8 jit_solution(141794151348740614)
XLA Ops:
  6.5 1.1 copy.12
  7.7 2.4 %collective-permute-start = (f32[3,128,2,128]{1,3,2,0:T(8,128)S(1)}, f32[3,128,2,128]{1,3,2,0:T(8,128)S(1)}, u32[]{:S(2)}, u32[]{:S(2)}) collective-permute-start(f32[3,128,2,128]{1,3,2,0:T(8,128)S(1)} %convert_element_type.32), channel_id=1, source_target_pairs={{0,8},{8,16},{16,24},{1,9},{9,17},{17,25},{2,10},{10,18},{18,26},{... | collective-permute-start | bytes 1179656 | tf_op jit(solution)/shard_map/ppermute | solution.py:20
  10.1 1.3 collective-permute-start.1
  11.4 0.7 fusion.39
  12.1 3.6 %collective-permute-done.1 = f32[3,128,2,128]{1,3,2,0:T(8,128)S(1)} collective-permute-done((f32[3,128,2,128]{1,3,2,0:T(8,128)S(1)}, f32[3,128,2,128]{1,3,2,0:T(8,128)S(1)}, u32[]{:S(2)}, u32[]{:S(2)}) %collective-permute-start.1) | collective-permute-done | bytes 393248 | tf_op jit(solution)/shard_map/ppermute | solution.py:23
  15.8 1.6 collective-permute-start.2
  17.4 3.2 %collective-permute-start.3 = (f32[3,128,6,2]{1,3,2,0:T(2,128)S(1)}, f32[3,128,6,2]{1,3,2,0:T(2,128)S(1)}, u32[]{:S(2)}, u32[]{:S(2)}) collective-permute-start(f32[3,128,6,2]{1,3,2,0:T(2,128)S(1)} %get-tuple-element.13), channel_id=1, source_target_pairs={{1,0},{2,1},{3,2},{4,3},{5,4},{6,5},{7,6},{0,7},{9,8},{10,9},{11,1... | collective-permute-start | bytes 55304 | tf_op jit(solution)/shard_map/ppermute | solution.py:23
  21.3 1.0 collective-permute-done.2
  22.3 0.1 pad_maximum_fusion
  22.4 0.1 slice_bitcast_fusion.1
  22.5 0.2 fusion.11
  22.8 0.2 pad_maximum_fusion.1
  23.0 0.1 fusion.21
  23.2 0.2 fusion.43
  23.4 1.9 %gather_fusion = f32[256,128]{1,0:T(8,128)S(1)} fusion(f32[3,128,256]{1,2,0:T(8,128)S(1)} %bitcast.80, s32[256]{0:T(256)S(1)} %bitcast.79), kind=kCustom, calls=%fused_computation | custom fusion | bytes 264192 | tf_op jit(solution)/shard_map/gather | solution.py:76
  25.3 0.1 reduce_sum.19
  25.4 1.2 fusion.26
  26.6 0.3 convolution_bitcast_fusion.2
  26.9 44.6 %psum.15 = f32[128]{0:T(128)S(1)} all-reduce(f32[128]{0:T(128)S(1)} %convolution_bitcast_fusion.2), channel_id=1, replica_groups=mesh['lat'=4,'lon'=8] {'lat','lon'}, use_global_device_ids=true, to_apply=%region_5.6 | all-reduce | flops 128 | bytes 1024 | tf_op jit(solution)/shard_map/psum | solution.py:86
  71.5 78.4 %all-reduce.2.cloned.1.call-done = f32[128,128]{1,0:T(8,128)} async-done(((f32[128,128]{1,0:T(8,128)}), f32[128,128]{1,0:T(8,128)}) %all-reduce.2.cloned.1.call-update) | async-done | bytes 65552 | tf_op jit(solution)/shard_map/psum | solution.py:86
  150.0 0.9 select_add_fusion
  150.8 0.1 copy.13
  150.9 0.9 fusion.31
  151.8 11.7 %cholesky.13 = f32[128,128]{1,0:T(8,128)S(1)} custom-call(f32[128,128]{1,0:T(8,128)S(1)} %fusion.31), custom_call_target="Cholesky" | custom-call | tf_op jit(solution)/shard_map/jit(cholesky)/cholesky | solution.py:87
  163.5 0.6 compare_reduce_fusion
  164.2 0.7 fusion.27
  164.8 9.8 %custom-call.10 = f32[1,128,128]{1,2,0:T(8,128)S(1)} custom-call(f32[1,128,128]{2,1,0:T(8,128)S(1)} %fusion.27), custom_call_target="InvertDiagBlocksLowerTriangular" | custom-call | tf_op jit(solution)/shard_map/triangular_solve | solution.py:88
  174.7 0.2 convolution_bitcast_fusion.1
  174.8 0.2 convolution_bitcast_fusion
  175.0 0.3 fusion.2
  175.3 0.7 fusion
  176.0 0.9 reshape.216
  (18 shorter events, 0.3 us)
Async XLA Ops:
  6.5 143.4 %all-reduce.2.cloned.1.call-start = ((), (), s32[]{:S(2)}) async-start(), calls=%async_computation | async-start | bytes 131072 | tf_op jit(solution)/shard_map/psum | solution.py:86
  7.7 4.5 %collective-permute-start = (f32[3,128,2,128]{1,3,2,0:T(8,128)S(1)}, f32[3,128,2,128]{1,3,2,0:T(8,128)S(1)}, u32[]{:S(2)}, u32[]{:S(2)}) collective-permute-start(f32[3,128,2,128]{1,3,2,0:T(8,128)S(1)} %convert_element_type.32), channel_id=1, source_target_pairs={{0,8},{8,16},{16,24},{1,9},{9,17},{17,25},{2,10},{10,18},{18,26},{... | collective-permute-start | bytes 1179656 | tf_op jit(solution)/shard_map/ppermute | solution.py:20
  10.1 5.7 %collective-permute-start.1 = (f32[3,128,2,128]{1,3,2,0:T(8,128)S(1)}, f32[3,128,2,128]{1,3,2,0:T(8,128)S(1)}, u32[]{:S(2)}, u32[]{:S(2)}) collective-permute-start(f32[3,128,2,128]{1,3,2,0:T(8,128)S(1)} %convert_element_type.32), channel_id=1, source_target_pairs={{8,0},{16,8},{24,16},{9,1},{17,9},{25,17},{10,2},{18,10},{26,18},{... | collective-permute-start | bytes 1179656 | tf_op jit(solution)/shard_map/ppermute | solution.py:23
  15.8 6.5 %collective-permute-start.2 = (f32[3,128,6,2]{1,3,2,0:T(2,128)S(1)}, f32[3,128,6,2]{1,3,2,0:T(2,128)S(1)}, u32[]{:S(2)}, u32[]{:S(2)}) collective-permute-start(f32[3,128,6,2]{1,3,2,0:T(2,128)S(1)} %get-tuple-element.12), channel_id=1, source_target_pairs={{0,1},{1,2},{2,3},{3,4},{4,5},{5,6},{6,7},{7,0},{8,9},{9,10},{10,1... | collective-permute-start | bytes 55304 | tf_op jit(solution)/shard_map/ppermute | solution.py:20
  17.4 4.9 %collective-permute-start.3 = (f32[3,128,6,2]{1,3,2,0:T(2,128)S(1)}, f32[3,128,6,2]{1,3,2,0:T(2,128)S(1)}, u32[]{:S(2)}, u32[]{:S(2)}) collective-permute-start(f32[3,128,6,2]{1,3,2,0:T(2,128)S(1)} %get-tuple-element.13), channel_id=1, source_target_pairs={{1,0},{2,1},{3,2},{4,3},{5,4},{6,5},{7,6},{0,7},{9,8},{10,9},{11,1... | collective-permute-start | bytes 55304 | tf_op jit(solution)/shard_map/ppermute | solution.py:23
  23.1 2.3 %copy-start = (f32[1,1,256]{2,1,0:T(1,128)S(1)}, f32[1,1,256]{2,1,0:T(1,128)}, u32[]{:S(2)}) copy-start(f32[1,1,256]{2,1,0:T(1,128)} %param.6) | copy-start | bytes 3076
  23.2 2.2 %copy-start.1 = (f32[1,1,256]{2,1,0:T(1,128)S(1)}, f32[1,1,256]{2,1,0:T(1,128)}, u32[]{:S(2)}) copy-start(f32[1,1,256]{2,1,0:T(1,128)} %param.7) | copy-start | bytes 3076
Sparse Core Ops, SparseCore 0:
  26.8 123.1 all-reduce.1
where the time goes:
time: 185 us; the launch traced here: 184 us
  waiting for transfers between devices  83.1 us (45%)
  blocking collectives  44.6 us (24%)
  other arithmetic  26.4 us (14%)
  between operations  14.2 us (8%)
  starting transfers between devices  8.45 us (5%)
  local copies, waits for them, and re-layouts  4.19 us (2%)
  matrix products  2.75 us (1%)
    psum x1, waiting for transfers between devices, shards(): gram, push = lax.psum((local_gram, local_push), ('lat', 'lon'))  78.4 us
    psum x1, blocking collectives, shards(): gram, push = lax.psum((local_gram, local_push), ('lat', 'lon'))  44.6 us
    another operation x3, other arithmetic, shards(): factor = jnp.linalg.cholesky(prior * identity + gram)  12.4 us
    another operation x2, other arithmetic, shards(): lax.linalg.triangular_solve(factor, identity, left_side=True, lower=True)  10.5 us
    ppermute x2, starting transfers between devices, with_halo(): lax.ppermute(lax.slice_in_dim(block, 0, width, axis=dim), axis, backward)  4.5 us
    ppermute x2, starting transfers between devices, with_halo(): lax.ppermute(lax.slice_in_dim(block, block.shape[dim] - width, None, axis...  3.95 us
  transfers between devices with their start and end apart: 5, of which 3 were waited for; matrix products, arithmetic and copies ran while one was open for 1% of the time, Pallas kernels for 0%

commit v1 on v0

v1 whole, which is shorter than its diff:
```python
import functools
import math

import jax
import jax.numpy as jnp
from jax import lax
from jax.experimental import pallas as pl
from jax.experimental.pallas import tpu as pltpu
from jax.sharding import PartitionSpec as P

HALF_COURANT = 0.4
ROTATION = 0.8
BAND = math.pi / 6.0
MESH = pl.DeviceIdType.MESH
F32 = jnp.float32
BF16 = jnp.bfloat16
HIGHEST = lax.Precision.HIGHEST
NT = (((1,), (1,)), ((), ()))
TN = (((0,), (0,)), ((), ()))
PANEL = 8


def split3(value):
    high = value.astype(BF16).astype(F32)
    rest = value - high
    middle = rest.astype(BF16).astype(F32)
    return high, middle, rest - middle


def forecast_kernel(
    n_lat, n_lon, prior, observed, obs_error, obs_index, obs_count,
    fields_out, total_out,
    wide, own, up_buf, down_buf, edges, from_low, from_high, cols, part, gathered, whole,
    send_sem, recv_sem, part_send, part_recv, whole_send, whole_recv,
):
    members = own.shape[1]
    lanes = own.shape[2]
    total = n_lat * n_lon
    lat = lax.axis_index("lat")
    lon = lax.axis_index("lon")
    me = lat * n_lon + lon
    east = lax.rem(lon + 1, n_lon)
    west = lax.rem(lon + n_lon - 1, n_lon)
    has_low = lat > 0
    has_high = lat < n_lat - 1
    chunks = part.shape[0]

    def place(index):
        return (index // n_lon, lax.rem(index, n_lon))

    def owner(chunk):
        line = 2 * (chunk // n_lon)
        return (line % n_lat + line // n_lat) * n_lon + chunk % n_lon

    barrier = pltpu.get_barrier_semaphore()

    def greet(step, carry):
        pl.semaphore_signal(
            barrier, inc=1, device_id=place(lax.rem(me + step, total)), device_id_type=MESH
        )
        return carry

    lax.fori_loop(1, total, greet, 0)

    wide[...] = prior[...].astype(F32)
    field_at = {"h": 0, "u": 1, "v": 2}
    slot_of = {"h": 0, "v": 1, "u": 2}
    state = {}
    for row in range(2):
        for name in "huv":
            block = wide[pl.ds(field_at[name] * 2 * members + row, members, stride=2), :]
            state[name, row] = block
            own[row * 3 + slot_of[name]] = block

    pick_row = lax.broadcasted_iota(jnp.int32, (8, lanes), 0)
    pick_col = lax.broadcasted_iota(jnp.int32, (8, lanes), 1)
    wanted = jnp.where(pick_row < 2, pick_row, pick_row + (lanes - 4))
    picker = jnp.where((pick_col == wanted) & (pick_row < 4), 1.0, 0.0).astype(BF16)
    for row in range(2):
        for at, name in enumerate("huv"):
            start = (row * 3 + at) * 8
            edges[start : start + 8, :] = lax.dot_general(
                picker, state[name, row].astype(BF16), NT, preferred_element_type=F32
            )

    lane = lax.broadcasted_iota(jnp.int32, (members, lanes), 1)
    first = lane == 0
    last = lane == lanes - 1
    zero = jnp.zeros((members, lanes), F32)

    def span(value, halo):
        ahead = jnp.where(last, halo, pltpu.roll(value, lanes - 1, 1))
        behind = jnp.where(first, halo, pltpu.roll(value, 1, 1))
        return ahead - behind

    rows = lat * 2 + lax.broadcasted_iota(jnp.int32, (8, lanes), 0)
    latitude = BAND * (2.0 * (rows.astype(F32) + 0.5) / (2 * n_lat) - 1.0)
    rotation = ROTATION * jnp.sin(latitude)
    rot = [rotation[row : row + 1, :] for row in range(2)]

    @pl.when(jnp.logical_not(has_low))
    def _():
        from_low[...] = jnp.zeros_like(from_low)
        cols[96:128, :] = jnp.zeros((32, members), F32)

    @pl.when(jnp.logical_not(has_high))
    def _():
        from_high[...] = jnp.zeros_like(from_high)
        cols[128:160, :] = jnp.zeros((32, members), F32)

    pl.semaphore_wait(barrier, total - 1)

    def copy(source, target, at, to):
        return pltpu.make_async_remote_copy(
            src_ref=source, dst_ref=target, send_sem=send_sem.at[at], recv_sem=recv_sem.at[at],
            device_id=to, device_id_type=MESH,
        )

    def rows_of(buf, start, count):
        return buf.at[pl.ds(start, count)]

    lon_copies = [
        copy(edges, rows_of(cols, 48, 48), 0, (lat, west)),
        copy(edges, rows_of(cols, 0, 48), 1, (lat, east)),
    ]
    low = lat - 1
    high = lat + 1
    low_copies = [
        copy(rows_of(own, 0, 2), rows_of(from_high, 0, 2), 2, (low, lon)),
        copy(down_buf, rows_of(from_high, 2, 2), 3, (low, lon)),
        copy(rows_of(edges, 8, 16), rows_of(cols, 144, 16), 4, (low, west)),
        copy(rows_of(edges, 8, 16), rows_of(cols, 128, 16), 5, (low, east)),
    ]
    high_copies = [
        copy(rows_of(own, 3, 2), rows_of(from_low, 0, 2), 6, (high, lon)),
        copy(up_buf, rows_of(from_low, 2, 2), 7, (high, lon)),
        copy(rows_of(edges, 32, 16), rows_of(cols, 112, 16), 8, (high, west)),
        copy(rows_of(edges, 32, 16), rows_of(cols, 96, 16), 9, (high, east)),
    ]

    @pl.when(has_high)
    def _():
        high_copies[0].start()

    @pl.when(has_low)
    def _():
        low_copies[0].start()

    for item in lon_copies:
        item.start()

    h0, u0, v0 = (state[name, 0] for name in "huv")
    h1, u1, v1 = (state[name, 1] for name in "huv")
    c = HALF_COURANT
    up_buf[0] = h1 - c * span(u1, zero) + c * v0
    up_buf[1] = v1 + c * h0 - rot[1] * u1
    down_buf[0] = h0 - c * span(u0, zero) - c * v1
    down_buf[1] = v0 - c * h1 - rot[0] * u0

    @pl.when(has_high)
    def _():
        for item in high_copies[1:]:
            item.start()

    @pl.when(has_low)
    def _():
        for item in low_copies[1:]:
            item.start()

    slots = observed.shape[1]
    slot = lax.broadcasted_iota(jnp.int32, (1, slots), 1)
    live = jnp.where(slot < obs_count[0, 0], 1.0, 0.0)
    scale = live / obs_error[...]
    squared = scale * scale
    pieces = split3(squared) + split3(squared * observed[...])
    pieces = jnp.concatenate(pieces + (jnp.zeros((2, slots), F32),), axis=0).astype(BF16)
    cells = 6 * lanes
    cell = lax.broadcasted_iota(jnp.int32, (cells, slots), 0)
    hits = jnp.where(cell == obs_index[...], 1.0, 0.0).astype(BF16)
    sums = lax.dot_general(pieces, hits, NT, preferred_element_type=F32)
    weight = sums[0:1] + sums[1:2] + sums[2:3]
    target = sums[3:4] + sums[4:5] + sums[5:6]

    for item in lon_copies:
        item.wait()

    @pl.when(has_high)
    def _():
        for item in high_copies:
            item.wait_send()
        for item in low_copies:
            item.wait_recv()

    @pl.when(has_low)
    def _():
        for item in low_copies:
            item.wait_send()
        for item in high_copies:
            item.wait_recv()

    ahead_t = cols[...].astype(BF16)
    key = lax.broadcasted_iota(jnp.int32, (160, lanes), 0)
    spot = lax.broadcasted_iota(jnp.int32, (160, lanes), 1)

    def halo(west_at, east_at):
        chosen = jnp.where(
            ((key == west_at) & (spot == 0)) | ((key == east_at) & (spot == lanes - 1)), 1.0, 0.0
        ).astype(BF16)
        return lax.dot_general(ahead_t, chosen, TN, preferred_element_type=F32)

    def near(name, row):
        if 0 <= row < 2:
            at = (row * 3 + "huv".index(name)) * 8
            return halo(at + 3, 48 + at)
        base = 96 if row < 0 else 128
        at = base + "uv".index(name) * 8
        return halo(at + 3, at + 16)

    def far(name, row):
        at = (row * 3 + "huv".index(name)) * 8
        return halo(at + 2, 48 + at + 1)

    side = jnp.where(first, -1.0, jnp.where(last, 1.0, 0.0))
    inside_low = jnp.where(has_low, 1.0, 0.0)
    inside_high = jnp.where(has_high, 1.0, 0.0)

    hm, vm, pm, qm = (from_low[at] for at in range(4))
    hp, vp, pp, qp = (from_high[at] for at in range(4))
    mid_h = {
        -1: pm - c * side * near("u", -1) - (c * inside_low) * v0,
        2: pp - c * side * near("u", 2) + (c * inside_high) * v1,
    }
    mid_v = {-1: qm - (c * inside_low) * h0, 2: qp + (c * inside_high) * h1}
    h = {-1: hm, 0: h0, 1: h1, 2: hp}
    v = {-1: vm, 0: v0, 1: v1, 2: vp}
    u = {0: u0, 1: u1}
    near_v = {row: near("v", row) for row in range(-1, 3)}
    rate = {}
    mid_u = {}
    edge_h = {}
    edge_u = {}
    for row in range(2):
        near_u = near("u", row)
        near_h = near("h", row)
        rate["h", row] = -c * (span(u[row], near_u) + (v[row + 1] - v[row - 1]))
        rate["u", row] = -c * span(h[row], near_h) + rot[row] * v[row]
        rate["v", row] = -c * (h[row + 1] - h[row - 1]) - rot[row] * u[row]
        mid_h[row] = h[row] + rate["h", row]
        mid_u[row] = u[row] + rate["u", row]
        mid_v[row] = v[row] + rate["v", row]
        edge_h[row] = near_h - c * (
            side * (far("u", row) - u[row]) + (near_v[row + 1] - near_v[row - 1])
        )
        edge_u[row] = near_u - c * side * (far("h", row) - h[row]) + rot[row] * near_v[row]

    centered = []
    shifts = []
    for at, name in enumerate("huv"):
        for row in range(2):
            if name == "h":
                second = -c * (span(mid_u[row], edge_u[row]) + (mid_v[row + 1] - mid_v[row - 1]))
            elif name == "u":
                second = -c * span(mid_h[row], edge_h[row]) + rot[row] * mid_v[row]
            else:
                second = -c * (mid_h[row + 1] - mid_h[row - 1]) - rot[row] * mid_u[row]
            value = state[name, row] + 0.5 * (rate[name, row] + second)
            center = jnp.sum(value, axis=0, keepdims=True) * (1.0 / members)
            block = slice((at * 2 + row) * lanes, (at * 2 + row + 1) * lanes)
            fields_out[0:members, block] = value - center
            fields_out[members : members + 8, block] = jnp.broadcast_to(center, (8, lanes))

    anomaly = fields_out[0:members, :]
    center = fields_out[members : members + 1, :]
    bottom = jnp.broadcast_to(target - weight * center, (8, cells))
    left = jnp.concatenate([anomaly * weight, bottom], axis=0)
    local = lax.dot_general(left, anomaly, NT, precision=HIGHEST, preferred_element_type=F32)
    for chunk in range(chunks):
        part[chunk] = local[chunk * 8 : chunk * 8 + 8, :]

    def part_copy(chunk):
        target_device = owner(chunk)
        distance = lax.rem(me - target_device + total, total)
        return pltpu.make_async_remote_copy(
            src_ref=part.at[chunk], dst_ref=gathered.at[distance - 1],
            send_sem=part_send.at[chunk], recv_sem=part_recv,
            device_id=place(target_device), device_id_type=MESH,
        )

    for chunk in range(chunks):
        @pl.when(owner(chunk) != me)
        def _():
            part_copy(chunk).start()

    def whole_copy(chunk, step):
        return pltpu.make_async_remote_copy(
            src_ref=whole.at[chunk], dst_ref=whole.at[chunk],
            send_sem=whole_send, recv_sem=whole_recv.at[chunk],
            device_id=place(lax.rem(me + step, total)), device_id_type=MESH,
        )

    for chunk in range(chunks):
        @pl.when(owner(chunk) == me)
        def _():
            pltpu.make_async_copy(gathered, gathered, part_recv).wait()
            whole[chunk] = part[chunk] + jnp.sum(gathered[...], axis=0)

            def send(step, carry):
                whole_copy(chunk, step).start()
                return carry

            lax.fori_loop(1, total, send, 0)

    for chunk in range(chunks):
        @pl.when(owner(chunk) != me)
        def _():
            part_copy(chunk).wait_send()
            whole_copy(chunk, 1).wait_recv()

        total_out[chunk * 8 : chunk * 8 + 8, :] = whole[chunk]

    for chunk in range(chunks):
        @pl.when(owner(chunk) == me)
        def _():
            pltpu.make_async_copy(gathered, gathered, whole_send).wait()


def update_kernel(fields, sums, out, work, inverse):
    members = work.shape[0]
    lanes = out.shape[1]
    prior = float(members - 1)
    row = lax.broadcasted_iota(jnp.int32, (members, members), 0)
    col = lax.broadcasted_iota(jnp.int32, (members, members), 1)
    work[...] = sums[0:members, :] + jnp.where(row == col, prior, 0.0)
    sub = lax.broadcasted_iota(jnp.int32, (PANEL, members), 0)
    at = lax.broadcasted_iota(jnp.int32, (PANEL, members), 1)
    for start in range(0, members, PANEL):
        stop = start + PANEL
        panel = work[start:stop, :]
        columns = [
            jnp.broadcast_to(panel[:, start + k : start + k + 1], (PANEL, members))
            for k in range(PANEL)
        ]
        reciprocal = jnp.zeros((PANEL, members), F32)
        for k in range(PANEL):
            over = 1.0 / columns[k][k : k + 1, :]
            reciprocal = jnp.where(sub == k, over, reciprocal)
            ratio = jnp.where(sub > k, columns[k] * over, 0.0)
            panel = jnp.where(at == start + k, jnp.where(sub == k, 1.0, jnp.where(sub > k, 0.0, panel)), panel)
            panel = panel - ratio * panel[k : k + 1, :]
            for j in range(k + 1, PANEL):
                columns[j] = columns[j] - ratio * columns[j][k : k + 1, :]
        inverse[start:stop, :] = jnp.where(at <= start + sub, panel, 0.0) * jnp.sqrt(reciprocal)
        if stop < members:
            ratios = panel * reciprocal
            used = jnp.where((at > start + sub) & (at < stop), 0.0, panel)
            change = lax.dot_general(
                ratios, used, TN, precision=HIGHEST, preferred_element_type=F32
            )
            below = work[stop:, :]
            keep = (col[stop:, :] < start) | (col[stop:, :] >= stop)
            work[stop:, :] = jnp.where(keep, below, 0.0) - change[stop:, :]
    lower = inverse[...]
    push = sums[members : members + 8, :]
    forward = lax.dot_general(push, lower, NT, precision=HIGHEST, preferred_element_type=F32)
    mean_weights = jnp.dot(forward, lower, precision=HIGHEST, preferred_element_type=F32)
    weights = math.sqrt(prior) * lower + mean_weights[0:1, :]
    anomaly = fields[0:members, :]
    center = fields[members : members + 1, :]
    result = center + jnp.dot(weights, anomaly, precision=HIGHEST, preferred_element_type=F32)
    for block in range(6):
        field, line = block // 2, block % 2
        out[pl.ds(field * 2 * members + line, members, stride=2), :] = result[
            :, block * lanes : (block + 1) * lanes
        ]


def shards(n_lat, n_lon, prior_ensemble, observed, obs_error, obs_index, obs_count):
    fields, members, rows, lanes = prior_ensemble.shape
    cells = fields * rows * lanes
    total = n_lat * n_lon
    chunks = members // 8 + 1
    vmem = pl.BlockSpec(memory_space=pltpu.VMEM)
    smem = pl.BlockSpec(memory_space=pltpu.SMEM)
    slots = observed.shape[-1]
    forecast, sums = pl.pallas_call(
        functools.partial(forecast_kernel, n_lat, n_lon),
        out_shape=(
            jax.ShapeDtypeStruct((members + 8, cells), F32),
            jax.ShapeDtypeStruct((members + 8, members), F32),
        ),
        in_specs=[vmem, vmem, vmem, vmem, smem],
        out_specs=(vmem, vmem),
        scratch_shapes=[
            pltpu.VMEM((fields * members * rows, lanes), F32),
            pltpu.VMEM((6, members, lanes), F32),
            pltpu.VMEM((2, members, lanes), F32),
            pltpu.VMEM((2, members, lanes), F32),
            pltpu.VMEM((48, members), F32),
            pltpu.VMEM((4, members, lanes), F32),
            pltpu.VMEM((4, members, lanes), F32),
            pltpu.VMEM((160, members), F32),
            pltpu.VMEM((chunks, 8, members), F32),
            pltpu.VMEM((total - 1, 8, members), F32),
            pltpu.VMEM((chunks, 8, members), F32),
            pltpu.SemaphoreType.DMA((10,)),
            pltpu.SemaphoreType.DMA((10,)),
            pltpu.SemaphoreType.DMA((chunks,)),
            pltpu.SemaphoreType.DMA,
            pltpu.SemaphoreType.DMA,
            pltpu.SemaphoreType.DMA((chunks,)),
        ],
        compiler_params=pltpu.CompilerParams(
            collective_id=0, has_side_effects=True, vmem_limit_bytes=32 * 1024 * 1024
        ),
    )(
        prior_ensemble.reshape(-1, lanes), observed.reshape(1, slots), obs_error.reshape(1, slots),
        obs_index.reshape(1, slots), obs_count,
    )
    out = pl.pallas_call(
        update_kernel,
        out_shape=jax.ShapeDtypeStruct((fields * members * rows, lanes), F32),
        in_specs=[vmem, vmem],
        out_specs=vmem,
        scratch_shapes=[
            pltpu.VMEM((members, members), F32),
            pltpu.VMEM((members, members), F32),
        ],
        compiler_params=pltpu.CompilerParams(vmem_limit_bytes=32 * 1024 * 1024),
    )(forecast, sums)
    return out.reshape(prior_ensemble.shape)


def solution(mesh):
    placed = (
        P(None, None, "lat", "lon"),
        P("lat", "lon", None),
        P("lat", "lon", None),
        P("lat", "lon", None),
        P("lat", "lon"),
    )
    return jax.shard_map(
        functools.partial(shards, mesh.shape["lat"], mesh.shape["lon"]),
        mesh=mesh, in_specs=placed, out_specs=P(None, None, "lat", "lon"), check_vma=False,
    )
```

time: 185 us -> 34.7 us (0.19)
  waiting for transfers between devices: 83.1 us -> 0 us
  blocking collectives: 44.6 us -> 0 us
  Pallas kernels: 0 us -> 32.3 us
  other arithmetic: 26.4 us -> 0 us
  between operations: 14.2 us -> 0.69 us
  starting transfers between devices: 8.45 us -> 0 us
  matrix products: 2.75 us -> 0 us
  local copies, waits for them, and re-layouts: 4.19 us -> 1.61 us
    psum x1 -> x0, waiting for transfers between devices: 78.4 us -> none  [shards(): gram, push = lax.psum((local_gram, local_push), ('lat', 'lon'))]
    psum x1 -> x0, blocking collectives: 44.6 us -> none  [shards(): gram, push = lax.psum((local_gram, local_push), ('lat', 'lon'))]
    pallas_call x0 -> x2, Pallas kernels: none -> 32.3 us  [the longest x1 23.3 us: shards(): pl.pallas_call(functools.partial(forecast_kernel, n_lat, n_lon), out_shap...]
    another operation x8 -> x0, other arithmetic: 23.4 us -> none  [the longest x3 12.4 us: shards(): factor = jnp.linalg.cholesky(prior * identity + gram)]
    ppermute x4 -> x0, starting transfers between devices: 8.45 us -> none  [the longest x2 4.5 us: with_halo(): lax.ppermute(lax.slice_in_dim(block, 0, width, axis=dim), axis, backward)]
    ppermute x4 -> x0, waiting for transfers between devices: 4.66 us -> none  [the longest x2 3.62 us: with_halo(): lax.ppermute(lax.slice_in_dim(block, 0, width, axis=dim), axis, backward)]
    dot_general x3 -> x0, matrix products: 2.1 us -> none  [the longest x1 1.17 us: shards(): local_gram = jnp.dot(scaled.T, scaled, precision=lax.Precision.HIGHEST)]
    gather x1 -> x0, local copies, waits for them, and re-layouts: 1.9 us -> none  [shards(): measured_vector = unrolled_vector[variable_slot, :, cell_index]]
  transfers between devices with their start and end apart: 5 -> 0, of which waited for: 3 -> 0; matrix products, arithmetic and copies ran while one was open for 1% -> 0% of each run, Pallas kernels for 0% -> 0%
where the time goes in v1:
time: 34.7 us; the launch traced here: 34.6 us
  Pallas kernels  32.3 us (93%)
  local copies, waits for them, and re-layouts  1.61 us (5%)
  between operations  0.69 us (2%)
    pallas_call x1, Pallas kernels, shards(): pl.pallas_call(functools.partial(forecast_kernel, n_lat, n_lon), out_shap...  23.3 us
    pallas_call x1, Pallas kernels, shards(): pl.pallas_call(update_kernel, out_shape=jax.ShapeDtypeStruct((fields * me...  8.96 us
    unnamed x8, local copies, waits for them, and re-layouts  1.61 us

profile of v1, /device:TPU:0, one launch (start us, length us, event | category | flops | bytes accessed | tf_op | source)
XLA Modules:
  0.0 34.6 jit_solution(1653184324243096731)
XLA Ops:
  0.7 0.0 copy-start.2
  0.7 0.0 copy-start.3
  0.7 0.0 copy-start.1
  0.7 0.7 %copy-done.2 = f32[1,1,256]{2,1,0:T(1,128)S(1)} copy-done((f32[1,1,256]{2,1,0:T(1,128)S(1)}, f32[1,1,256]{2,1,0:T(1,128)}, u32[]{:S(2)}) %copy-start.2) | copy-done | bytes 1048
  1.3 0.0 copy-done.3
  1.3 0.0 copy-done.1
  1.4 0.0 copy-start
  1.4 0.9 %copy-done = bf16[3,128,2,128]{3,2,1,0:T(2,128)(2,1)S(1)} copy-done((bf16[3,128,2,128]{3,2,1,0:T(2,128)(2,1)S(1)}, bf16[3,128,2,128]{3,2,1,0:T(2,128)(2,1)}, u32[]{:S(2)}) %copy-start) | copy-done | bytes 196632
  2.3 23.3 %shard_map.55 = (f32[136,768]{1,0:T(8,128)S(1)}, f32[136,128]{1,0:T(8,128)S(1)}) custom-call(bf16[768,128]{1,0:T(8,128)(2,1)S(1)} %bitcast.5, f32[1,256]{1,0:T(1,128)S(1)} %bitcast.6, f32[1,256]{1,0:T(1,128)S(1)} %bitcast.7, s32[1,256]{1,0:T(1,128)S(1)} %bitcast.8, s32[1,1]{1,0:T(1,128)S(6)} %copy.6.obs_count), custom_call_target="tpu_custom_call" | custom-call | tf_op jit(solution)/shard_map/pallas_call | solution.py:385
  25.6 9.0 %shard_map.56 = f32[768,128]{1,0:T(8,128)} custom-call(f32[136,768]{1,0:T(8,128)S(1)} %get-tuple-element.7.fields, f32[136,128]{1,0:T(8,128)S(1)} %get-tuple-element.8.sums), custom_call_target="tpu_custom_call" | custom-call | tf_op jit(solution)/shard_map/pallas_call | solution.py:419
Async XLA Ops:
  0.7 0.7 %copy-start.2 = (f32[1,1,256]{2,1,0:T(1,128)S(1)}, f32[1,1,256]{2,1,0:T(1,128)}, u32[]{:S(2)}) copy-start(f32[1,1,256]{2,1,0:T(1,128)} %param.7) | copy-start | bytes 3076
  0.7 0.7 %copy-start.3 = (s32[1,1,256]{2,1,0:T(1,128)S(1)}, s32[1,1,256]{2,1,0:T(1,128)}, u32[]{:S(2)}) copy-start(s32[1,1,256]{2,1,0:T(1,128)} %param.8) | copy-start | bytes 3076
  0.7 0.7 %copy-start.1 = (f32[1,1,256]{2,1,0:T(1,128)S(1)}, f32[1,1,256]{2,1,0:T(1,128)}, u32[]{:S(2)}) copy-start(f32[1,1,256]{2,1,0:T(1,128)} %param.6) | copy-start | bytes 3076
  1.4 0.9 %copy-start = (bf16[3,128,2,128]{3,2,1,0:T(2,128)(2,1)S(1)}, bf16[3,128,2,128]{3,2,1,0:T(2,128)(2,1)}, u32[]{:S(2)}) copy-start(bf16[3,128,2,128]{3,2,1,0:T(2,128)(2,1)} %param.5) | copy-start | bytes 589828

commit v2 on v1

--- a/solution.py
+++ b/solution.py
@@ -17,7 +17,8 @@
 HIGHEST = lax.Precision.HIGHEST
 NT = (((1,), (1,)), ((), ()))
 TN = (((0,), (0,)), ((), ()))
-PANEL = 8
+PANEL = 16
+VMEM_LIMIT = 56 * 1024 * 1024
 
 
 def split3(value):
@@ -28,8 +29,9 @@
 
 
 def forecast_kernel(
-    n_lat, n_lon, prior, observed, obs_error, obs_index, obs_count,
+    n_lat, n_lon, prior_in, observed_in, obs_error_in, obs_index_in, count_in,
     fields_out, total_out,
+    prior, observed, obs_error, obs_index, obs_count, in_sem,
     wide, own, up_buf, down_buf, edges, from_low, from_high, cols, part, gathered, whole,
     send_sem, recv_sem, part_send, part_recv, whole_send, whole_recv,
 ):
@@ -52,6 +54,17 @@
         line = 2 * (chunk // n_lon)
         return (line % n_lat + line // n_lat) * n_lon + chunk % n_lon
 
+    fetches = [
+        pltpu.make_async_copy(source, target, in_sem.at[at])
+        for at, (source, target) in enumerate(
+            (
+                (prior_in, prior), (observed_in, observed), (obs_error_in, obs_error),
+                (obs_index_in, obs_index), (count_in, obs_count),
+            )
+        )
+    ]
+    for item in fetches:
+        item.start()
     barrier = pltpu.get_barrier_semaphore()
 
     def greet(step, carry):
@@ -61,6 +74,7 @@
         return carry
 
     lax.fori_loop(1, total, greet, 0)
+    fetches[0].wait()
 
     wide[...] = prior[...].astype(F32)
     field_at = {"h": 0, "u": 1, "v": 2}
@@ -138,16 +152,18 @@
         copy(rows_of(edges, 32, 16), rows_of(cols, 96, 16), 9, (high, east)),
     ]
 
-    @pl.when(has_high)
-    def _():
-        high_copies[0].start()
-
-    @pl.when(has_low)
-    def _():
-        low_copies[0].start()
-
     for item in lon_copies:
         item.start()
+
+    @pl.when(has_high)
+    def _():
+        for at in (2, 3, 0):
+            high_copies[at].start()
+
+    @pl.when(has_low)
+    def _():
+        for at in (2, 3, 0):
+            low_copies[at].start()
 
     h0, u0, v0 = (state[name, 0] for name in "huv")
     h1, u1, v1 = (state[name, 1] for name in "huv")
@@ -159,14 +175,14 @@
 
     @pl.when(has_high)
     def _():
-        for item in high_copies[1:]:
-            item.start()
+        high_copies[1].start()
 
     @pl.when(has_low)
     def _():
-        for item in low_copies[1:]:
-            item.start()
-
+        low_copies[1].start()
+
+    for item in fetches[1:]:
+        item.wait()
     slots = observed.shape[1]
     slot = lax.broadcasted_iota(jnp.int32, (1, slots), 1)
     live = jnp.where(slot < obs_count[0, 0], 1.0, 0.0)
@@ -186,16 +202,12 @@
 
     @pl.when(has_high)
     def _():
-        for item in high_copies:
-            item.wait_send()
-        for item in low_copies:
+        for item in low_copies[2:]:
             item.wait_recv()
 
     @pl.when(has_low)
     def _():
-        for item in low_copies:
-            item.wait_send()
-        for item in high_copies:
+        for item in high_copies[2:]:
             item.wait_recv()
 
     ahead_t = cols[...].astype(BF16)
@@ -224,15 +236,13 @@
     inside_low = jnp.where(has_low, 1.0, 0.0)
     inside_high = jnp.where(has_high, 1.0, 0.0)
 
-    hm, vm, pm, qm = (from_low[at] for at in range(4))
-    hp, vp, pp, qp = (from_high[at] for at in range(4))
     mid_h = {
-        -1: pm - c * side * near("u", -1) - (c * inside_low) * v0,
-        2: pp - c * side * near("u", 2) + (c * inside_high) * v1,
+        -1: -c * side * near("u", -1) - (c * inside_low) * v0,
+        2: -c * side * near("u", 2) + (c * inside_high) * v1,
     }
-    mid_v = {-1: qm - (c * inside_low) * h0, 2: qp + (c * inside_high) * h1}
-    h = {-1: hm, 0: h0, 1: h1, 2: hp}
-    v = {-1: vm, 0: v0, 1: v1, 2: vp}
+    mid_v = {-1: -(c * inside_low) * h0, 2: (c * inside_high) * h1}
+    h = {-1: zero, 0: h0, 1: h1, 2: zero}
+    v = {-1: zero, 0: v0, 1: v1, 2: zero}
     u = {0: u0, 1: u1}
     near_v = {row: near("v", row) for row in range(-1, 3)}
     rate = {}
@@ -253,8 +263,6 @@
         )
         edge_u[row] = near_u - c * side * (far("h", row) - h[row]) + rot[row] * near_v[row]
 
-    centered = []
-    shifts = []
     for at, name in enumerate("huv"):
         for row in range(2):
             if name == "h":
@@ -264,6 +272,36 @@
             else:
                 second = -c * (mid_h[row + 1] - mid_h[row - 1]) - rot[row] * mid_u[row]
             value = state[name, row] + 0.5 * (rate[name, row] + second)
+            wide[pl.ds((at * 2 + row) * members, members), :] = value
+
+    @pl.when(has_high)
+    def _():
+        for item in high_copies:
+            item.wait_send()
+        for item in low_copies[:2]:
+            item.wait_recv()
+
+    @pl.when(has_low)
+    def _():
+        for item in low_copies:
+            item.wait_send()
+        for item in high_copies[:2]:
+            item.wait_recv()
+
+    hm, vm, pm, qm = (from_low[at] for at in range(4))
+    hp, vp, pp, qp = (from_high[at] for at in range(4))
+    half = 0.5 * c
+    more = {
+        ("h", 0): half * (vm + qm + c * hp),
+        ("h", 1): half * (c * hm - vp - qp),
+        ("u", 0): half * (rot[0] * hm - c * span(vm, zero)),
+        ("u", 1): half * (c * span(vp, zero) - rot[1] * hp),
+        ("v", 0): half * (hm + pm + c * vp),
+        ("v", 1): half * (c * vm - hp - pp),
+    }
+    for at, name in enumerate("huv"):
+        for row in range(2):
+            value = wide[pl.ds((at * 2 + row) * members, members), :] + more[name, row]
             center = jnp.sum(value, axis=0, keepdims=True) * (1.0 / members)
             block = slice((at * 2 + row) * lanes, (at * 2 + row + 1) * lanes)
             fields_out[0:members, block] = value - center
@@ -291,37 +329,48 @@
         def _():
             part_copy(chunk).start()
 
-    def whole_copy(chunk, step):
+    def whole_copy(chunk, to):
         return pltpu.make_async_remote_copy(
             src_ref=whole.at[chunk], dst_ref=whole.at[chunk],
             send_sem=whole_send, recv_sem=whole_recv.at[chunk],
-            device_id=place(lax.rem(me + step, total)), device_id_type=MESH,
+            device_id=to, device_id_type=MESH,
         )
 
-    for chunk in range(chunks):
-        @pl.when(owner(chunk) == me)
-        def _():
-            pltpu.make_async_copy(gathered, gathered, part_recv).wait()
-            whole[chunk] = part[chunk] + jnp.sum(gathered[...], axis=0)
-
-            def send(step, carry):
-                whole_copy(chunk, step).start()
-                return carry
-
-            lax.fori_loop(1, total, send, 0)
+    mine = [owner(chunk) == me for chunk in range(chunks)]
+    my_chunk = sum(jnp.where(mine[chunk], chunk, 0) for chunk in range(chunks))
+    owns = functools.reduce(jnp.logical_or, mine)
+
+    @pl.when(owns)
+    def _():
+        pltpu.make_async_copy(gathered, gathered, part_recv).wait()
+        whole[my_chunk] = part[my_chunk] + jnp.sum(gathered[...], axis=0)
+
+        def send_lat(step, start):
+            to_lat = lax.rem(lat + step, n_lat)
+            to_lon = lax.rem(lon + start, n_lon)
+            for _ in range(start, n_lon):
+                whole_copy(my_chunk, (to_lat, to_lon)).start()
+                to_lon = jnp.where(to_lon == n_lon - 1, 0, to_lon + 1)
+
+        def send(step, carry):
+            send_lat(step, 0)
+            return carry
+
+        lax.fori_loop(1, n_lat, send, 0)
+        send_lat(0, 1)
 
     for chunk in range(chunks):
         @pl.when(owner(chunk) != me)
         def _():
             part_copy(chunk).wait_send()
-            whole_copy(chunk, 1).wait_recv()
-
+            whole_copy(chunk, (lat, east)).wait_recv()
+
+    for chunk in range(chunks):
         total_out[chunk * 8 : chunk * 8 + 8, :] = whole[chunk]
 
-    for chunk in range(chunks):
-        @pl.when(owner(chunk) == me)
-        def _():
-            pltpu.make_async_copy(gathered, gathered, whole_send).wait()
+    @pl.when(owns)
+    def _():
+        pltpu.make_async_copy(gathered, gathered, whole_send).wait()
 
 
 def update_kernel(fields, sums, out, work, inverse):
@@ -344,11 +393,13 @@
         for k in range(PANEL):
             over = 1.0 / columns[k][k : k + 1, :]
             reciprocal = jnp.where(sub == k, over, reciprocal)
-            ratio = jnp.where(sub > k, columns[k] * over, 0.0)
-            panel = jnp.where(at == start + k, jnp.where(sub == k, 1.0, jnp.where(sub > k, 0.0, panel)), panel)
-            panel = panel - ratio * panel[k : k + 1, :]
+            below = jnp.where(sub > k, columns[k], 0.0)
+            panel = jnp.where(
+                at == start + k, jnp.where(sub == k, 1.0, jnp.where(sub > k, 0.0, panel)), panel
+            )
+            panel = panel - (below * panel[k : k + 1, :]) * over
             for j in range(k + 1, PANEL):
-                columns[j] = columns[j] - ratio * columns[j][k : k + 1, :]
+                columns[j] = columns[j] - (below * columns[j][k : k + 1, :]) * over
         inverse[start:stop, :] = jnp.where(at <= start + sub, panel, 0.0) * jnp.sqrt(reciprocal)
         if stop < members:
             ratios = panel * reciprocal
@@ -380,7 +431,6 @@
     total = n_lat * n_lon
     chunks = members // 8 + 1
     vmem = pl.BlockSpec(memory_space=pltpu.VMEM)
-    smem = pl.BlockSpec(memory_space=pltpu.SMEM)
     slots = observed.shape[-1]
     forecast, sums = pl.pallas_call(
         functools.partial(forecast_kernel, n_lat, n_lon),
@@ -388,9 +438,15 @@
             jax.ShapeDtypeStruct((members + 8, cells), F32),
             jax.ShapeDtypeStruct((members + 8, members), F32),
         ),
-        in_specs=[vmem, vmem, vmem, vmem, smem],
+        in_specs=[pl.BlockSpec(memory_space=pl.ANY)] * 5,
         out_specs=(vmem, vmem),
         scratch_shapes=[
+            pltpu.VMEM((fields * members * rows, lanes), prior_ensemble.dtype),
+            pltpu.VMEM((1, slots), F32),
+            pltpu.VMEM((1, slots), F32),
+            pltpu.VMEM((1, slots), jnp.int32),
+            pltpu.SMEM((1, 1), jnp.int32),
+            pltpu.SemaphoreType.DMA((5,)),
             pltpu.VMEM((fields * members * rows, lanes), F32),
             pltpu.VMEM((6, members, lanes), F32),
             pltpu.VMEM((2, members, lanes), F32),
@@ -410,7 +466,7 @@
             pltpu.SemaphoreType.DMA((chunks,)),
         ],
         compiler_params=pltpu.CompilerParams(
-            collective_id=0, has_side_effects=True, vmem_limit_bytes=32 * 1024 * 1024
+            collective_id=0, has_side_effects=True, vmem_limit_bytes=VMEM_LIMIT
         ),
     )(
         prior_ensemble.reshape(-1, lanes), observed.reshape(1, slots), obs_error.reshape(1, slots),
@@ -425,7 +481,7 @@
             pltpu.VMEM((members, members), F32),
             pltpu.VMEM((members, members), F32),
         ],
-        compiler_params=pltpu.CompilerParams(vmem_limit_bytes=32 * 1024 * 1024),
+        compiler_params=pltpu.CompilerParams(vmem_limit_bytes=VMEM_LIMIT),
     )(forecast, sums)
     return out.reshape(prior_ensemble.shape)
 

time: 34.7 us -> 31.7 us (0.914)
  local copies, waits for them, and re-layouts: 1.61 us -> 0 us
  Pallas kernels: 32.3 us -> 30.9 us
    pallas_call x1, Pallas kernels: 8.96 us -> 7.06 us  [shards(): pl.pallas_call(update_kernel, out_shape=jax.ShapeDtypeStruct((fields * me...]
    unnamed x8 -> x0, local copies, waits for them, and re-layouts: 1.61 us -> none
    pallas_call x1, Pallas kernels: 23.3 us -> 23.9 us  [shards(): pl.pallas_call(functools.partial(forecast_kernel, n_lat, n_lon), out_shap...]
where the time goes in v2:
time: 31.7 us; the launch traced here: 31.6 us
  Pallas kernels  30.9 us (97%)
  between operations  0.66 us (2%)
    pallas_call x1, Pallas kernels, shards(): pl.pallas_call(functools.partial(forecast_kernel, n_lat, n_lon), out_shap...  23.9 us
    pallas_call x1, Pallas kernels, shards(): pl.pallas_call(update_kernel, out_shape=jax.ShapeDtypeStruct((fields * me...  7.06 us

profile of v2, /device:TPU:0, one launch (start us, length us, event | category | flops | bytes accessed | tf_op | source)
XLA Modules:
  0.0 31.6 jit_solution(4493339691087665095)
XLA Ops:
  0.7 23.9 %shard_map.55 = (f32[136,768]{1,0:T(8,128)}, f32[136,128]{1,0:T(8,128)}) custom-call(bf16[768,128]{1,0:T(8,128)(2,1)} %bitcast.5, f32[1,256]{1,0:T(1,128)} %bitcast.6, f32[1,256]{1,0:T(1,128)} %bitcast.7, s32[1,256]{1,0:T(1,128)} %bitcast.8, s32[1,1]{1,0:T(1,128)S(6)} %copy.6.count_in), custom_call_target="tpu_custom_call" | custom-call | tf_op jit(solution)/shard_map/pallas_call | solution.py:435
  24.5 7.1 %shard_map.56 = f32[768,128]{1,0:T(8,128)} custom-call(f32[136,768]{1,0:T(8,128)} %get-tuple-element.7.fields, f32[136,128]{1,0:T(8,128)} %get-tuple-element.8.sums), custom_call_target="tpu_custom_call" | custom-call | tf_op jit(solution)/shard_map/pallas_call | solution.py:475

commit v3 on v2

--- a/solution.py
+++ b/solution.py
@@ -17,7 +17,7 @@
 HIGHEST = lax.Precision.HIGHEST
 NT = (((1,), (1,)), ((), ()))
 TN = (((0,), (0,)), ((), ()))
-PANEL = 16
+PANEL = 32
 VMEM_LIMIT = 56 * 1024 * 1024
 
 
@@ -30,8 +30,8 @@
 
 def forecast_kernel(
     n_lat, n_lon, prior_in, observed_in, obs_error_in, obs_index_in, count_in,
-    fields_out, total_out,
-    prior, observed, obs_error, obs_index, obs_count, in_sem,
+    fields_hbm, center_hbm, total_out,
+    fields, centers, gram_left, out_sem, prior, observed, obs_error, obs_index, obs_count, in_sem,
     wide, own, up_buf, down_buf, edges, from_low, from_high, cols, part, gathered, whole,
     send_sem, recv_sem, part_send, part_recv, whole_send, whole_recv,
 ):
@@ -210,7 +210,7 @@
         for item in high_copies[2:]:
             item.wait_recv()
 
-    ahead_t = cols[...].astype(BF16)
+    ahead = cols[...].T.astype(BF16)
     key = lax.broadcasted_iota(jnp.int32, (160, lanes), 0)
     spot = lax.broadcasted_iota(jnp.int32, (160, lanes), 1)
 
@@ -218,7 +218,7 @@
         chosen = jnp.where(
             ((key == west_at) & (spot == 0)) | ((key == east_at) & (spot == lanes - 1)), 1.0, 0.0
         ).astype(BF16)
-        return lax.dot_general(ahead_t, chosen, TN, preferred_element_type=F32)
+        return jnp.dot(ahead, chosen, preferred_element_type=F32)
 
     def near(name, row):
         if 0 <= row < 2:
@@ -304,14 +304,34 @@
             value = wide[pl.ds((at * 2 + row) * members, members), :] + more[name, row]
             center = jnp.sum(value, axis=0, keepdims=True) * (1.0 / members)
             block = slice((at * 2 + row) * lanes, (at * 2 + row + 1) * lanes)
-            fields_out[0:members, block] = value - center
-            fields_out[members : members + 8, block] = jnp.broadcast_to(center, (8, lanes))
-
-    anomaly = fields_out[0:members, :]
-    center = fields_out[members : members + 1, :]
-    bottom = jnp.broadcast_to(target - weight * center, (8, cells))
-    left = jnp.concatenate([anomaly * weight, bottom], axis=0)
-    local = lax.dot_general(left, anomaly, NT, precision=HIGHEST, preferred_element_type=F32)
+            anomaly = value - center
+            above = anomaly.astype(BF16)
+            fields[0:members, block] = above
+            fields[members:, block] = (anomaly - above.astype(F32)).astype(BF16)
+            centers[:, block] = jnp.broadcast_to(center, (8, lanes))
+            share = weight[:, block]
+            scaled = jnp.concatenate(
+                [
+                    anomaly * share,
+                    jnp.broadcast_to(target[:, block] - share * center, (16, lanes)),
+                ],
+                axis=0,
+            )
+            above = scaled.astype(BF16)
+            gram_left[0, :, block] = above
+            gram_left[1, :, block] = (scaled - above.astype(F32)).astype(BF16)
+
+    fields_copy = pltpu.make_async_copy(fields, fields_hbm, out_sem.at[0])
+    center_copy = pltpu.make_async_copy(centers, center_hbm, out_sem.at[1])
+    fields_copy.start()
+    center_copy.start()
+
+    def product(left, right):
+        return lax.dot_general(left, right, NT, preferred_element_type=F32)
+
+    local = product(gram_left[0], fields[0:members, :])
+    local += product(gram_left[0], fields[members:, :])
+    local += product(gram_left[1], fields[0:members, :])
     for chunk in range(chunks):
         part[chunk] = local[chunk * 8 : chunk * 8 + 8, :]
 
@@ -372,38 +392,75 @@
     def _():
         pltpu.make_async_copy(gathered, gathered, whole_send).wait()
 
-
-def update_kernel(fields, sums, out, work, inverse):
+    fields_copy.wait()
+    center_copy.wait()
+
+
+def inverse_of(pivot):
+    guess = pl.reciprocal(pivot, approx=True)
+    guess = guess * (2.0 - pivot * guess)
+    return guess * (2.0 - pivot * guess)
+
+
+def update_kernel(
+    fields_hbm, center_hbm, sums, out_hbm, fields, centers, out, work, inverse, in_sem, out_sem
+):
+    fetches = [
+        pltpu.make_async_copy(fields_hbm, fields, in_sem.at[0]),
+        pltpu.make_async_copy(center_hbm, centers, in_sem.at[1]),
+    ]
+    for item in fetches:
+        item.start()
     members = work.shape[0]
     lanes = out.shape[1]
     prior = float(members - 1)
     row = lax.broadcasted_iota(jnp.int32, (members, members), 0)
     col = lax.broadcasted_iota(jnp.int32, (members, members), 1)
     work[...] = sums[0:members, :] + jnp.where(row == col, prior, 0.0)
-    sub = lax.broadcasted_iota(jnp.int32, (PANEL, members), 0)
-    at = lax.broadcasted_iota(jnp.int32, (PANEL, members), 1)
+    sub = lax.broadcasted_iota(jnp.int32, (8, members), 0)
+    at = lax.broadcasted_iota(jnp.int32, (8, members), 1)
+    groups = PANEL // 8
     for start in range(0, members, PANEL):
         stop = start + PANEL
-        panel = work[start:stop, :]
-        columns = [
-            jnp.broadcast_to(panel[:, start + k : start + k + 1], (PANEL, members))
+        panel = [work[start + 8 * g : start + 8 * g + 8, :] for g in range(groups)]
+        columns = {
+            (g, k): jnp.broadcast_to(panel[g][:, start + k : start + k + 1], (8, members))
+            for g in range(groups)
             for k in range(PANEL)
-        ]
-        reciprocal = jnp.zeros((PANEL, members), F32)
+        }
+        reciprocal = [jnp.zeros((8, members), F32) for _ in range(groups)]
         for k in range(PANEL):
-            over = 1.0 / columns[k][k : k + 1, :]
-            reciprocal = jnp.where(sub == k, over, reciprocal)
-            below = jnp.where(sub > k, columns[k], 0.0)
-            panel = jnp.where(
-                at == start + k, jnp.where(sub == k, 1.0, jnp.where(sub > k, 0.0, panel)), panel
+            own, line = k // 8, k % 8
+            over = inverse_of(columns[own, k][line : line + 1, :])
+            reciprocal[own] = jnp.where(sub == line, over, reciprocal[own])
+            here = at == start + k
+            pivot = jnp.where(here[0:1, :], 1.0, panel[own][line : line + 1, :])
+            factors = {j: columns[own, j][line : line + 1, :] for j in range(k + 1, PANEL)}
+            for g in range(own, groups):
+                below = columns[g, k]
+                if g == own:
+                    below = jnp.where(sub > line, below, 0.0)
+                    cleared = jnp.where(
+                        here, jnp.where(sub == line, 1.0, jnp.where(sub > line, 0.0, panel[g])), panel[g]
+                    )
+                else:
+                    cleared = jnp.where(here, 0.0, panel[g])
+                panel[g] = cleared - (below * pivot) * over
+                for j in range(k + 1, PANEL):
+                    columns[g, j] = columns[g, j] - (below * factors[j]) * over
+        for g in range(groups):
+            inverse[start + 8 * g : start + 8 * g + 8, :] = jnp.where(
+                at <= start + 8 * g + sub, panel[g], 0.0
+            ) * jnp.sqrt(reciprocal[g])
+        if stop < members:
+            ratios = jnp.concatenate([panel[g] * reciprocal[g] for g in range(groups)], axis=0)
+            used = jnp.concatenate(
+                [
+                    jnp.where((at > start + 8 * g + sub) & (at < stop), 0.0, panel[g])
+                    for g in range(groups)
+                ],
+                axis=0,
             )
-            panel = panel - (below * panel[k : k + 1, :]) * over
-            for j in range(k + 1, PANEL):
-                columns[j] = columns[j] - (below * columns[j][k : k + 1, :]) * over
-        inverse[start:stop, :] = jnp.where(at <= start + sub, panel, 0.0) * jnp.sqrt(reciprocal)
-        if stop < members:
-            ratios = panel * reciprocal
-            used = jnp.where((at > start + sub) & (at < stop), 0.0, panel)
             change = lax.dot_general(
                 ratios, used, TN, precision=HIGHEST, preferred_element_type=F32
             )
@@ -415,14 +472,27 @@
     forward = lax.dot_general(push, lower, NT, precision=HIGHEST, preferred_element_type=F32)
     mean_weights = jnp.dot(forward, lower, precision=HIGHEST, preferred_element_type=F32)
     weights = math.sqrt(prior) * lower + mean_weights[0:1, :]
-    anomaly = fields[0:members, :]
-    center = fields[members : members + 1, :]
-    result = center + jnp.dot(weights, anomaly, precision=HIGHEST, preferred_element_type=F32)
-    for block in range(6):
-        field, line = block // 2, block % 2
-        out[pl.ds(field * 2 * members + line, members, stride=2), :] = result[
-            :, block * lanes : (block + 1) * lanes
-        ]
+    above = weights.astype(BF16)
+    rest = (weights - above.astype(F32)).astype(BF16)
+    twice = jnp.concatenate([above, above], axis=1)
+    for item in fetches:
+        item.wait()
+    copies = []
+    for field in range(3):
+        block = slice(field * 2 * lanes, (field + 1) * 2 * lanes)
+        result = centers[0:1, block] + (
+            jnp.dot(twice, fields[:, block], preferred_element_type=F32)
+            + jnp.dot(rest, fields[0:members, block], preferred_element_type=F32)
+        )
+        for line in range(2):
+            out[pl.ds(field * 2 * members + line, members, stride=2), :] = result[
+                :, line * lanes : (line + 1) * lanes
+            ]
+        span = pl.ds(field * 2 * members, 2 * members)
+        copies.append(pltpu.make_async_copy(out.at[span], out_hbm.at[span], out_sem.at[field]))
+        copies[-1].start()
+    for item in copies:
+        item.wait()
 
 
 def shards(n_lat, n_lon, prior_ensemble, observed, obs_error, obs_index, obs_count):
@@ -432,15 +502,21 @@
     chunks = members // 8 + 1
     vmem = pl.BlockSpec(memory_space=pltpu.VMEM)
     slots = observed.shape[-1]
-    forecast, sums = pl.pallas_call(
+    hbm = pl.BlockSpec(memory_space=pl.ANY)
+    forecast, center, sums = pl.pallas_call(
         functools.partial(forecast_kernel, n_lat, n_lon),
         out_shape=(
-            jax.ShapeDtypeStruct((members + 8, cells), F32),
+            jax.ShapeDtypeStruct((2 * members, cells), BF16),
+            jax.ShapeDtypeStruct((8, cells), F32),
             jax.ShapeDtypeStruct((members + 8, members), F32),
         ),
-        in_specs=[pl.BlockSpec(memory_space=pl.ANY)] * 5,
-        out_specs=(vmem, vmem),
+        in_specs=[hbm] * 5,
+        out_specs=(hbm, hbm, vmem),
         scratch_shapes=[
+            pltpu.VMEM((2 * members, cells), BF16),
+            pltpu.VMEM((8, cells), F32),
+            pltpu.VMEM((2, members + 16, cells), BF16),
+            pltpu.SemaphoreType.DMA((2,)),
             pltpu.VMEM((fields * members * rows, lanes), prior_ensemble.dtype),
             pltpu.VMEM((1, slots), F32),
             pltpu.VMEM((1, slots), F32),
@@ -475,14 +551,19 @@
     out = pl.pallas_call(
         update_kernel,
         out_shape=jax.ShapeDtypeStruct((fields * members * rows, lanes), F32),
-        in_specs=[vmem, vmem],
-        out_specs=vmem,
+        in_specs=[hbm, hbm, vmem],
+        out_specs=hbm,
         scratch_shapes=[
+            pltpu.VMEM((2 * members, cells), BF16),
+            pltpu.VMEM((8, cells), F32),
+            pltpu.VMEM((fields * members * rows, lanes), F32),
             pltpu.VMEM((members, members), F32),
             pltpu.VMEM((members, members), F32),
+            pltpu.SemaphoreType.DMA((2,)),
+            pltpu.SemaphoreType.DMA((3,)),
         ],
         compiler_params=pltpu.CompilerParams(vmem_limit_bytes=VMEM_LIMIT),
-    )(forecast, sums)
+    )(forecast, center, sums)
     return out.reshape(prior_ensemble.shape)
 
 

time: 31.7 us -> 32.1 us (1.013)
    pallas_call x1, Pallas kernels: 7.06 us -> 7.63 us  [shards(): pl.pallas_call(update_kernel, out_shape=jax.ShapeDtypeStruct((fields * me...]
where the time goes in v3:
time: 32.1 us; the launch traced here: 31.9 us
  Pallas kernels  31.2 us (97%)
  between operations  0.66 us (2%)
    pallas_call x1, Pallas kernels, shards(): pl.pallas_call(functools.partial(forecast_kernel, n_lat, n_lon), out_shap...  23.6 us
    pallas_call x1, Pallas kernels, shards(): pl.pallas_call(update_kernel, out_shape=jax.ShapeDtypeStruct((fields * me...  7.63 us

profile of v3, /device:TPU:0, one launch (start us, length us, event | category | flops | bytes accessed | tf_op | source)
XLA Modules:
  0.0 31.9 jit_solution(14244784991698883712)
XLA Ops:
  0.7 23.6 %shard_map.55 = (bf16[256,768]{1,0:T(8,128)(2,1)}, f32[8,768]{1,0:T(8,128)}, f32[136,128]{1,0:T(8,128)}) custom-call(bf16[768,128]{1,0:T(8,128)(2,1)} %bitcast.5, f32[1,256]{1,0:T(1,128)} %bitcast.6, f32[1,256]{1,0:T(1,128)} %bitcast.7, s32[1,256]{1,0:T(1,128)} %bitcast.8, s32[1,1]{1,0:T(1,128)S(6)} %copy.6.count_in), custom_call_target="tpu_custom_call" | custom-call | tf_op jit(solution)/shard_map/pallas_call | solution.py:506
  24.2 7.6 %shard_map.56 = f32[768,128]{1,0:T(8,128)} custom-call(bf16[256,768]{1,0:T(8,128)(2,1)} %get-tuple-element.8.fields_hbm, f32[8,768]{1,0:T(8,128)} %get-tuple-element.9.center_hbm, f32[136,128]{1,0:T(8,128)} %get-tuple-element.10.sums), custom_call_target="tpu_custom_call" | custom-call | tf_op jit(solution)/shard_map/pallas_call | solution.py:551
